TPU v7x, 256 devices: a whole 4x4x8 slice. The times are simulated.
256 devices in a mesh: inst: 32 (over x, z_hi, core), head: 8 (over y, z_lo).
Axes of the slice: x: 4, y: 4, z: 8 (z_hi: 4, z_lo: 2; z = z_hi * 2 + z_lo), core: 2. Of those that a mesh axis runs over, the one named last changes fastest.
Arguments:
- kv_cache: bfloat16 [768, 2, 128, 512], P('inst', None, None, 'head'), may hold values from -5 to 5
- query: bfloat16 [768, 8192], P('inst', 'head'), may hold values from -120 to 120
- fresh_kv: bfloat16 [768, 1024], P('inst', 'head'), may hold values from -5 to 5
- lengths: int32 [768], replicated, may hold values from 1 to 128, 49152 in all
- owner: int32 [768, 1], replicated, may hold values from 0 to 31; in each aligned block of 24 rows (0 to 23, 24 to 47, ...) at most 2 rows name the same one
- tokens: bfloat16 [4096, 4096], P(('inst', 'head')), may hold values from -6 to 6
- expert_ids: int32 [4096, 8], P(('inst', 'head')), may hold values from 0 to 127, all different within a row; in each aligned block of 16 rows (0 to 15, 16 to 31, ...) at most 2 rows name the same one
- gate_weights: float32 [4096, 8], P(('inst', 'head')), may hold values from 0.1 to 0.5
- w_gate: bfloat16 [98304, 4096], P(('inst', 'head')), may hold values from -0.09375 to 0.09375
- w_up: bfloat16 [98304, 4096], P(('inst', 'head')), may hold values from -0.09375 to 0.09375
- w_down: bfloat16 [98304, 4096], P(('inst', 'head')), may hold values from -0.21875 to 0.21875
Outputs:
- handed_cache: bfloat16 [2048, 2, 128, 512], P(('inst', 'head'))
- attention: bfloat16 [2048, 8192], P(('inst', 'head'))
- moe_out: bfloat16 [4096, 4096], P(('inst', 'head'))
Inputs may be any that keep to these rules, and one draw needn't show every extreme that they name: `owner`: in each aligned block of 24 prompts no decode instance is named more than 2 times, and some decode instance exactly 2 times. `expert_ids`: each row names 8 different experts; among the rows of one device (aligned blocks of 16 rows) no expert is named more than 2 times, a bound that some block reaches.
All inputs are finite; a program needn't handle non-finite values.
Results may differ from a plain program's by a relative error of at most 0.015.
Values may be sent and summed in bfloat16 or wider, within the bound.
A program may use at most 128 MiB of HBM per device.

v0:
```python
import jax
import jax.numpy as jnp
from jax import lax
from jax.sharding import PartitionSpec as P

QUERY_HEADS = 64
KEY_VALUE_HEADS = 4
HEAD_DIM_SIZE = 128
EXP_INST = 4


def slot_index(owner_rows, target, capacity):
    matches_dest = (owner_rows == target).astype(jnp.int32)
    ranking = jnp.cumsum(matches_dest, axis=-1) - 1
    slot_ids = jnp.arange(capacity, dtype=jnp.int32)
    matched = (matches_dest[..., None] == 1) & (ranking[..., None] == slot_ids)
    row_ids = jnp.arange(owner_rows.shape[-1], dtype=jnp.int32)
    chosen = jnp.sum(jnp.where(matched, row_ids[:, None], 0), axis=-2)
    return (chosen, jnp.any(matched, axis=-2))


def decode_attention(query_rows, handed_over, newest_rows, slot_length):
    count_of_slots = query_rows.shape[0]
    prompt_length = handed_over.shape[2]
    query_groups = QUERY_HEADS // KEY_VALUE_HEADS
    score_scale = HEAD_DIM_SIZE ** (-0.5)
    query_head_count = query_rows.reshape(
        count_of_slots, KEY_VALUE_HEADS, query_groups, HEAD_DIM_SIZE
    )
    every_key = handed_over[:, 0].reshape(
        count_of_slots, prompt_length, KEY_VALUE_HEADS, HEAD_DIM_SIZE
    )
    every_value = handed_over[:, 1].reshape(
        count_of_slots, prompt_length, KEY_VALUE_HEADS, HEAD_DIM_SIZE
    )
    newest_keys = newest_rows[:, : KEY_VALUE_HEADS * HEAD_DIM_SIZE].reshape(
        count_of_slots, KEY_VALUE_HEADS, HEAD_DIM_SIZE
    )
    newest_values = newest_rows[:, KEY_VALUE_HEADS * HEAD_DIM_SIZE :].reshape(
        count_of_slots, KEY_VALUE_HEADS, HEAD_DIM_SIZE
    )
    scores = (
        jnp.einsum(
            "skgd,sjkd->skgj", query_head_count, every_key, preferred_element_type=jnp.float32
        )
        * score_scale
    )
    own_score = (
        jnp.einsum(
            "skgd,skd->skg", query_head_count, newest_keys, preferred_element_type=jnp.float32
        )
        * score_scale
    )
    live_mask = (jnp.arange(prompt_length)[None, :] < slot_length[:, None])[:, None, None, :]
    highest = jnp.maximum(jnp.max(jnp.where(live_mask, scores, -1e30), axis=-1), own_score)
    exp_terms = jnp.where(live_mask, jnp.exp(scores - highest[..., None]), 0.0)
    own_exp = jnp.exp(own_score - highest)
    totals = jnp.sum(exp_terms, axis=-1) + own_exp
    weights = (exp_terms / totals[..., None]).astype(jnp.bfloat16)
    own_weight = (own_exp / totals).astype(jnp.bfloat16)
    mixed_out = jnp.einsum(
        "skgj,sjkd->skgd", weights, every_value, preferred_element_type=jnp.float32
    )
    mixed_out = (
        mixed_out
        + own_weight.astype(jnp.float32)[..., None]
        * newest_values.astype(jnp.float32)[:, :, None, :]
    )
    return mixed_out.reshape(count_of_slots, QUERY_HEADS * HEAD_DIM_SIZE).astype(jnp.bfloat16)


def local(
    kv_cache,
    query,
    fresh_kv,
    lengths,
    owner,
    tokens,
    expert_ids,
    gate_weights,
    w_gate,
    w_up,
    w_down,
):
    inst_count = lax.axis_size("inst")
    head_count = lax.axis_size("head")
    inst_pos = lax.axis_index("inst")
    head_pos = lax.axis_index("head")
    prompt_count = kv_cache.shape[0]
    seq_len = kv_cache.shape[2]
    capacity = max(2, (2 * prompt_count + inst_count - 1) // inst_count)
    owner_grid = owner[:, 0].reshape(inst_count, prompt_count)
    length_grid = lengths.reshape(inst_count, prompt_count)
    own_owner = lax.dynamic_index_in_dim(owner_grid, inst_pos, 0, keepdims=False)
    own_length = lax.dynamic_index_in_dim(length_grid, inst_pos, 0, keepdims=False)
    targets = jnp.arange(inst_count, dtype=jnp.int32)[:, None]
    send_rows, send_valid = slot_index(own_owner[None, :], targets, capacity)
    send_rows = send_rows.reshape(-1)
    send_valid = send_valid.reshape(-1)
    positions = jnp.arange(seq_len, dtype=jnp.int32)
    live_pos = positions[None, :] < own_length[:, None]
    masked = jnp.where(live_pos[:, None, :, None], kv_cache, jnp.zeros((), kv_cache.dtype))
    packed_cache = jnp.where(
        send_valid[:, None, None, None],
        jnp.take(masked, send_rows, axis=0),
        jnp.zeros((), kv_cache.dtype),
    )
    token_rows = jnp.concatenate([query, fresh_kv], axis=1)
    packed_tokens = jnp.where(
        send_valid[:, None],
        jnp.take(token_rows, send_rows, axis=0),
        jnp.zeros((), token_rows.dtype),
    )[:, None, None, :]
    handed_over, arrived = (
        lax.all_to_all(
            lax.all_to_all(packed_cache, "inst", split_axis=0, concat_axis=0, tiled=True),
            "head",
            split_axis=0,
            concat_axis=3,
            tiled=True,
        ),
        lax.all_to_all(
            lax.all_to_all(packed_tokens, "inst", split_axis=0, concat_axis=0, tiled=True),
            "head",
            split_axis=0,
            concat_axis=3,
            tiled=True,
        ),
    )
    block_count = inst_count // head_count
    src_owner = lax.dynamic_slice_in_dim(owner_grid, head_pos * block_count, block_count, 0)
    src_length = lax.dynamic_slice_in_dim(length_grid, head_pos * block_count, block_count, 0)
    recv_rows, recv_valid = slot_index(src_owner, inst_pos, capacity)
    slot_length = jnp.where(
        recv_valid, jnp.take_along_axis(src_length, recv_rows, axis=1), 0
    ).reshape(-1)
    count_of_slots = handed_over.shape[0]
    pieces = arrived.reshape(count_of_slots, head_count, -1)
    query_width = query.shape[1]
    query_rows = pieces[:, :, :query_width].reshape(count_of_slots, -1)
    newest_rows = pieces[:, :, query_width:].reshape(count_of_slots, -1)
    attention = decode_attention(query_rows, handed_over, newest_rows, slot_length)
    token_count = tokens.shape[0]
    model_width = tokens.shape[1]
    expert_count = inst_count * EXP_INST
    expert_cap = max(2, (16 * token_count + expert_count - 1) // expert_count)
    picked_hot = expert_ids[:, :, None] == jnp.arange(expert_count, dtype=jnp.int32)[None, None, :]
    counts_hot = jnp.sum(picked_hot.astype(jnp.int32), axis=1)
    ranking = jnp.cumsum(counts_hot, axis=0) - 1
    slot_ids = jnp.arange(expert_cap, dtype=jnp.int32)
    matched = (counts_hot[:, :, None] == 1) & (ranking[:, :, None] == slot_ids)
    token_ids = jnp.arange(token_count, dtype=jnp.int32)
    pick_rows = jnp.sum(jnp.where(matched, token_ids[:, None, None], 0), axis=0)
    pick_valid = jnp.any(matched, axis=0)
    outgoing = jnp.where(
        pick_valid.reshape(-1)[:, None],
        jnp.take(tokens, pick_rows.reshape(-1), axis=0),
        jnp.zeros((), tokens.dtype),
    )
    copies = max(1, head_count // EXP_INST)
    per_head = max(1, EXP_INST // head_count)
    outgoing = outgoing.reshape(inst_count, EXP_INST, expert_cap, model_width)
    outgoing = jnp.repeat(outgoing, copies, axis=1)
    outgoing = outgoing.reshape(inst_count, head_count, per_head, expert_cap, model_width)
    incoming = lax.all_to_all(
        lax.all_to_all(outgoing, "inst", split_axis=0, concat_axis=0, tiled=True),
        "head",
        split_axis=1,
        concat_axis=1,
        tiled=True,
    )
    unit_count = w_gate.shape[0]
    gate_rows = w_gate.reshape(per_head, unit_count // per_head, model_width)
    up_rows = w_up.reshape(per_head, unit_count // per_head, model_width)
    down_rows = w_down.reshape(per_head, unit_count // per_head, model_width)
    gate_val = jnp.einsum(
        "ihecd,eud->ihecu", incoming, gate_rows, preferred_element_type=jnp.float32
    )
    up_val = jnp.einsum("ihecd,eud->ihecu", incoming, up_rows, preferred_element_type=jnp.float32)
    hidden = (jax.nn.silu(gate_val) * up_val).astype(jnp.bfloat16)
    partial_value = jnp.einsum(
        "ihecu,eud->ihecd", hidden, down_rows, preferred_element_type=jnp.float32
    )
    returned = lax.all_to_all(
        lax.all_to_all(
            partial_value.astype(jnp.bfloat16), "inst", split_axis=0, concat_axis=0, tiled=True
        ),
        "head",
        split_axis=1,
        concat_axis=1,
        tiled=True,
    ).astype(partial_value.dtype)
    returned = returned.reshape(inst_count, EXP_INST, copies, expert_cap, model_width)
    expert_out = jnp.sum(returned, axis=2).astype(jnp.bfloat16)
    expert_out = expert_out.reshape(expert_count * expert_cap, model_width).astype(jnp.float32)
    rank_pick = jnp.sum(jnp.where(picked_hot, ranking[:, None, :], 0), axis=2)
    flat_slot = expert_ids * expert_cap + rank_pick
    gathered = jnp.take(expert_out, flat_slot.reshape(-1), axis=0).reshape(
        token_count, expert_ids.shape[1], model_width
    )
    moe_out = jnp.sum(gate_weights[:, :, None] * gathered, axis=1).astype(jnp.bfloat16)
    return (handed_over, attention, moe_out)


def solution(mesh):
    in_specs = (
        P("inst", None, None, "head"),
        P("inst", "head"),
        P("inst", "head"),
        P(),
        P(),
        P(("inst", "head"), None),
        P(("inst", "head"), None),
        P(("inst", "head"), None),
        P(("inst", "head"), None),
        P(("inst", "head"), None),
        P(("inst", "head"), None),
    )
    out_specs = (
        P(("inst", "head"), None, None, None),
        P(("inst", "head"), None),
        P(("inst", "head"), None),
    )
    return jax.shard_map(local, mesh=mesh, in_specs=in_specs, out_specs=out_specs, check_vma=False)
```

profile of v0, /device:TPU:2, one launch (start us, length us, event | category | flops | bytes accessed | tf_op | source)
XLA Modules:
  0.0 504.7 jit_solution(10859846438271845426)
XLA Ops:
  0.7 0.8 reduce.1
  1.6 0.8 reshape.409
  4.0 0.8 pad_maximum_fusion
  4.9 0.7 gather_fusion.1
  5.6 0.8 fusion.39
  6.9 1.6 reduce.3
  9.3 11.6 %all-to-all-start.2 = ((bf16[32,2,1152]{2,1,0:T(2,128)(2,1)}), bf16[32,2,1152]{2,1,0:T(2,128)(2,1)S(1)}, u32[]{:S(2)}, u32[]{:S(2)}) async-start(bf16[32,2,1152]{2,1,0:T(2,128)(2,1)} %reshape.468), calls=%async_computation.2 | async-start | bytes 294912 | tf_op jit(solution)/shard_map/all_to_all | solution.py:123
  22.5 0.8 reshape.414
  23.2 1.3 fusion.50
  25.9 3.2 gather_fusion.2
  29.1 4.4 gather.34
  33.9 4.3 broadcast_select_fusion.1
  38.3 2.0 copy.184
  40.3 4.7 broadcast_in_dim.219
  45.0 7.2 %reshape_reshape.7 = bf16[32,8,1,2,4096]{4,1,3,2,0:T(8,128)(2,1)} reshape(bf16[32,4,2,2,4096]{4,2,1,3,0:T(2,128)(2,1)} %broadcast_in_dim.219) | data formatting | bytes 8388608 | tf_op jit(solution)/shard_map/reshape;reshape | solution.py:164
  52.9 9.8 %all-to-all-start.4 = ((bf16[32,8,1,2,4096]{4,1,3,2,0:T(8,128)(2,1)}), bf16[32,8,1,2,4096]{4,1,3,2,0:T(8,128)(2,1)}, u32[]{:S(2)}, u32[]{:S(2)}) async-start(bf16[32,8,1,2,4096]{4,1,3,2,0:T(8,128)(2,1)} %reshape_reshape.7), calls=%async_computation.4 | async-start | bytes 8388608 | tf_op jit(solution)/shard_map/all_to_all | solution.py:166
  62.7 1.4 reshape.469
  64.2 2.2 reduce.4
  66.3 1.6 reshape.470
  68.0 86.2 %all-to-all-done.4 = bf16[32,8,1,2,4096]{4,1,3,2,0:T(8,128)(2,1)} async-done(((bf16[32,8,1,2,4096]{4,1,3,2,0:T(8,128)(2,1)}), bf16[32,8,1,2,4096]{4,1,3,2,0:T(8,128)(2,1)}, u32[]{:S(2)}, u32[]{:S(2)}) %all-to-all-start.4) | async-done | bytes 4194336 | tf_op jit(solution)/shard_map/all_to_all | solution.py:166
  154.2 6.3 %all-to-all-start.3 = ((bf16[8,2,4608]{2,1,0:T(2,128)(2,1)}), bf16[8,2,4608]{2,1,0:T(2,128)(2,1)S(1)}, u32[]{:S(2)}, u32[]{:S(2)}) async-start(bf16[8,2,4608]{2,1,0:T(2,128)(2,1)} %reshape.470), calls=%async_computation.3 | async-start | bytes 294912 | tf_op jit(solution)/shard_map/all_to_all | solution.py:122
  160.5 8.5 %copy.185 = bf16[32,8,1,2,4096]{4,3,0,2,1:T(2,128)(2,1)} copy(bf16[32,8,1,2,4096]{4,1,3,2,0:T(8,128)(2,1)} %all-to-all-done.4) | data formatting | bytes 8388608 | tf_op jit(solution)/shard_map/all_to_all | solution.py:166
  169.0 5.7 %all-to-all-start.5 = ((bf16[32,8,1,2,4096]{4,3,0,2,1:T(2,128)(2,1)}), bf16[32,8,1,2,4096]{4,3,0,2,1:T(2,128)(2,1)}, u32[]{:S(2)}, u32[]{:S(2)}) async-start(bf16[32,8,1,2,4096]{4,3,0,2,1:T(2,128)(2,1)} %copy.185), calls=%async_computation.5 | async-start | bytes 8388608 | tf_op jit(solution)/shard_map/all_to_all | solution.py:165
  174.8 2.1 broadcast_select_fusion.2
  177.0 3.4 gather_fusion
  180.4 3.2 select_select_fusion
  183.6 39.5 %all-to-all-done.5 = bf16[32,8,1,2,4096]{4,3,0,2,1:T(2,128)(2,1)} async-done(((bf16[32,8,1,2,4096]{4,3,0,2,1:T(2,128)(2,1)}), bf16[32,8,1,2,4096]{4,3,0,2,1:T(2,128)(2,1)}, u32[]{:S(2)}, u32[]{:S(2)}) %all-to-all-start.5) | async-done | bytes 4194336 | tf_op jit(solution)/shard_map/all_to_all | solution.py:165
  223.1 10.9 %all-to-all-start = ((bf16[64,2,128,64]{2,3,1,0:T(8,128)(2,1)}), bf16[64,2,128,64]{2,3,1,0:T(8,128)(2,1)}, u32[]{:S(2)}, u32[]{:S(2)}) async-start(bf16[64,2,128,64]{2,3,1,0:T(8,128)(2,1)} %select_select_fusion), calls=%async_computation | async-start | bytes 4194304 | tf_op jit(solution)/shard_map/all_to_all | solution.py:116
  233.9 6.0 %fusion.12 = f32[32,8,1,2,384]{4,1,3,0,2:T(8,128)S(1)} fusion(bf16[384,4096]{1,0:T(8,128)(2,1)} %param.19, bf16[32,8,1,2,4096]{4,3,0,2,1:T(2,128)(2,1)} %all-to-all-done.5), kind=kOutput, calls=%fused_computation.24 | convolution fusion | flops 1610612736 | bytes 8126464 | tf_op jit(solution)/shard_map/ihecd,eud->ihecu/dot_general | solution.py:176
  240.0 5.1 %fusion.32 = bf16[32,8,2,384]{3,1,2,0:T(8,128)(2,1)S(1)} fusion(bf16[384,4096]{1,0:T(8,128)(2,1)S(1)} %copy-done.17, bf16[32,8,1,2,4096]{4,3,0,2,1:T(2,128)(2,1)} %all-to-all-done.5, f32[32,8,1,2,384]{4,1,3,0,2:T(8,128)S(1)} %fusion.12), kind=kOutput, calls=%fused_computation.28 | convolution fusion | flops 1611792384 | bytes 8519680 | tf_op jit(solution)/shard_map/ihecd,eud->ihecu/dot_general | solution.py:179
  245.1 4.3 fusion
  249.4 34.6 %all-to-all-done = bf16[64,2,128,64]{2,3,1,0:T(8,128)(2,1)} async-done(((bf16[64,2,128,64]{2,3,1,0:T(8,128)(2,1)}), bf16[64,2,128,64]{2,3,1,0:T(8,128)(2,1)}, u32[]{:S(2)}, u32[]{:S(2)}) %all-to-all-start) | async-done | bytes 2097184 | tf_op jit(solution)/shard_map/all_to_all | solution.py:116
  284.0 101.5 %all_to_all.63 = bf16[32,8,1,2,4096]{4,1,3,2,0:T(8,128)(2,1)} all-to-all(bf16[32,8,1,2,4096]{4,1,3,2,0:T(8,128)(2,1)} %fusion), channel_id=1, replica_groups=mesh['inst'=32,'head'=8] {'inst'}, dimensions={0} | all-to-all | bytes 8388608 | tf_op jit(solution)/shard_map/all_to_all | solution.py:185
  385.5 3.8 all-to-all-start.1
  389.3 8.5 %copy.188 = bf16[32,8,1,2,4096]{4,3,0,2,1:T(2,128)(2,1)} copy(bf16[32,8,1,2,4096]{4,1,3,2,0:T(8,128)(2,1)} %all_to_all.63) | data formatting | bytes 8388608 | tf_op jit(solution)/shard_map/all_to_all | solution.py:185
  397.8 19.4 %all-to-all-done.1 = bf16[64,2,128,64]{2,3,1,0:T(8,128)(2,1)S(1)} async-done(((bf16[64,2,128,64]{2,3,1,0:T(8,128)(2,1)}), bf16[64,2,128,64]{2,3,1,0:T(8,128)(2,1)S(1)}, u32[]{:S(2)}, u32[]{:S(2)}) %all-to-all-start.1) | async-done | bytes 2097184 | tf_op jit(solution)/shard_map/all_to_all | solution.py:115
  417.2 1.3 copy-done.3
  418.5 4.5 all-to-all-start.7
  426.7 1.8 copy.170
  428.6 2.6 copy.192
  432.8 0.8 copy.229
  433.6 39.1 %all-to-all-done.7 = bf16[32,8,1,2,4096]{4,3,0,2,1:T(2,128)(2,1)} async-done(((bf16[32,8,1,2,4096]{4,3,0,2,1:T(2,128)(2,1)}), bf16[32,8,1,2,4096]{4,3,0,2,1:T(2,128)(2,1)}, u32[]{:S(2)}, u32[]{:S(2)}) %all-to-all-start.7) | async-done | bytes 4194336 | tf_op jit(solution)/shard_map/all_to_all | solution.py:184
  472.7 9.6 %bitcast_reduce_fusion = bf16[32,4,2,4096]{3,2,0,1:T(2,128)(2,1)S(1)} fusion(bf16[32,4,2,2,4096]{4,3,0,2,1:T(2,128)(2,1)} %bitcast.129), kind=kLoop, calls=%fused_computation.7 | loop fusion | flops 1048576 | bytes 6291456 | tf_op jit(solution)/shard_map/reduce_sum | solution.py:194
  482.3 1.7 copy_convert_fusion
  484.0 5.2 %copy.191 = f32[32,4,2,4096]{3,2,1,0:T(2,128)} copy(f32[32,4,2,4096]{3,0,2,1:T(8,128)S(1)} %copy_convert_fusion) | data formatting | bytes 8388608 | tf_op jit(solution)/shard_map/convert_element_type | solution.py:195
  489.2 6.3 %reshape.422 = f32[256,4096]{1,0:T(8,128)} reshape(f32[32,4,2,4096]{3,2,1,0:T(2,128)} %copy.191) | data formatting | bytes 8388608 | tf_op jit(solution)/shard_map/convert_element_type | solution.py:195
  495.5 5.8 %gather_fusion.3 = f32[128,4096]{1,0:T(8,128)} fusion(f32[256,4096]{1,0:T(8,128)} %reshape.422, s32[1024]{0:T(1024)S(1)} %pad_clamp_fusion), kind=kCustom, calls=%fused_computation.3 | custom fusion | bytes 4194816 | tf_op jit(solution)/shard_map/jit(_take)/gather | solution.py:198
  501.3 3.0 fusion.11
  (107 shorter events, 12.3 us)
Async XLA Ops:
  0.6 244.5 %copy-start = (bf16[384,4096]{1,0:T(8,128)(2,1)S(1)}, bf16[384,4096]{1,0:T(8,128)(2,1)}, u32[]{:S(2)}) copy-start(bf16[384,4096]{1,0:T(8,128)(2,1)} %param.21) | copy-start | bytes 9437188
  0.6 20.3 %copy-start.11 = (s32[16,8]{0,1:T(8,128)S(1)}, s32[16,8]{0,1:T(8,128)}, u32[]{:S(2)}) copy-start(s32[16,8]{0,1:T(8,128)} %param.17) | copy-start | bytes 1540
  0.7 25.2 %copy-start.2 = (bf16[16,4096]{1,0:T(8,128)(2,1)S(1)}, bf16[16,4096]{1,0:T(8,128)(2,1)}, u32[]{:S(2)}) copy-start(bf16[16,4096]{1,0:T(8,128)(2,1)} %param.16) | copy-start | bytes 393220
  1.6 1.4 copy-start.5
  3.8 17.4 %copy-start.8 = (s32[1024]{0:T(1024)}, s32[1024]{0:T(1024)S(1)}, u32[]{:S(2)}) copy-start(s32[1024]{0:T(1024)S(1)} %pad_clamp_fusion.2) | copy-start | bytes 12292
  3.8 17.3 %copy-start.13 = (pred[64]{0:T(512)(128)(4,1)}, pred[64]{0:T(512)(128)(4,1)S(1)}, u32[]{:S(2)}) copy-start(pred[64]{0:T(512)(128)(4,1)S(1)} %compare_and_fusion.2) | copy-start | bytes 196
  4.0 17.2 %copy-start.9 = (pred[64]{0:T(512)(128)(4,1)}, pred[64]{0:T(512)(128)(4,1)S(1)}, u32[]{:S(2)}) copy-start(pred[64]{0:T(512)(128)(4,1)S(1)} %broadcast_in_dim.191) | copy-start | bytes 196
  9.3 42.9 %all-to-all-start.2 = ((bf16[32,2,1152]{2,1,0:T(2,128)(2,1)}), bf16[32,2,1152]{2,1,0:T(2,128)(2,1)S(1)}, u32[]{:S(2)}, u32[]{:S(2)}) async-start(bf16[32,2,1152]{2,1,0:T(2,128)(2,1)} %reshape.468), calls=%async_computation.2 | async-start | bytes 294912 | tf_op jit(solution)/shard_map/all_to_all | solution.py:123
  21.1 0.6 copy-start.6
  21.8 0.6 copy-start.7
  29.1 4.7 copy-start.16
  52.2 0.7 copy-start.4
  52.9 101.3 %all-to-all-start.4 = ((bf16[32,8,1,2,4096]{4,1,3,2,0:T(8,128)(2,1)}), bf16[32,8,1,2,4096]{4,1,3,2,0:T(8,128)(2,1)}, u32[]{:S(2)}, u32[]{:S(2)}) async-start(bf16[32,8,1,2,4096]{4,1,3,2,0:T(8,128)(2,1)} %reshape_reshape.7), calls=%async_computation.4 | async-start | bytes 8388608 | tf_op jit(solution)/shard_map/all_to_all | solution.py:166
  154.2 14.8 %all-to-all-start.3 = ((bf16[8,2,4608]{2,1,0:T(2,128)(2,1)}), bf16[8,2,4608]{2,1,0:T(2,128)(2,1)S(1)}, u32[]{:S(2)}, u32[]{:S(2)}) async-start(bf16[8,2,4608]{2,1,0:T(2,128)(2,1)} %reshape.470), calls=%async_computation.3 | async-start | bytes 294912 | tf_op jit(solution)/shard_map/all_to_all | solution.py:122
  169.0 5.7 %copy-start.15 = (s32[24]{0:T(128)S(1)}, s32[24]{0:T(128)}, u32[]{:S(2)}) copy-start(s32[24]{0:T(128)} %get-tuple-element.42) | copy-start | bytes 292
  169.0 54.0 %all-to-all-start.5 = ((bf16[32,8,1,2,4096]{4,3,0,2,1:T(2,128)(2,1)}), bf16[32,8,1,2,4096]{4,3,0,2,1:T(2,128)(2,1)}, u32[]{:S(2)}, u32[]{:S(2)}) async-start(bf16[32,8,1,2,4096]{4,3,0,2,1:T(2,128)(2,1)} %copy.185), calls=%async_computation.5 | async-start | bytes 8388608 | tf_op jit(solution)/shard_map/all_to_all | solution.py:165
  177.0 3.4 copy-start.10
  177.0 3.4 copy-start.14
  223.1 60.9 %all-to-all-start = ((bf16[64,2,128,64]{2,3,1,0:T(8,128)(2,1)}), bf16[64,2,128,64]{2,3,1,0:T(8,128)(2,1)}, u32[]{:S(2)}, u32[]{:S(2)}) async-start(bf16[64,2,128,64]{2,3,1,0:T(8,128)(2,1)} %select_select_fusion), calls=%async_computation | async-start | bytes 4194304 | tf_op jit(solution)/shard_map/all_to_all | solution.py:116
  233.9 6.1 %copy-start.17 = (bf16[384,4096]{1,0:T(8,128)(2,1)S(1)}, bf16[384,4096]{1,0:T(8,128)(2,1)}, u32[]{:S(2)}) copy-start(bf16[384,4096]{1,0:T(8,128)(2,1)} %param.20) | copy-start | bytes 9437188
  385.5 31.7 %all-to-all-start.1 = ((bf16[64,2,128,64]{2,3,1,0:T(8,128)(2,1)}), bf16[64,2,128,64]{2,3,1,0:T(8,128)(2,1)S(1)}, u32[]{:S(2)}, u32[]{:S(2)}) async-start(bf16[64,2,128,64]{2,3,1,0:T(8,128)(2,1)} %all-to-all-done), calls=%async_computation.1 | async-start | bytes 4194304 | tf_op jit(solution)/shard_map/all_to_all | solution.py:115
  397.8 27.6 %copy-start.12 = (f32[16,8]{0,1:T(8,128)S(1)}, f32[16,8]{0,1:T(8,128)}, u32[]{:S(2)}) copy-start(f32[16,8]{0,1:T(8,128)} %param.18) | copy-start | bytes 1540
  417.2 1.3 copy-start.3
  418.5 54.2 %all-to-all-start.7 = ((bf16[32,8,1,2,4096]{4,3,0,2,1:T(2,128)(2,1)}), bf16[32,8,1,2,4096]{4,3,0,2,1:T(2,128)(2,1)}, u32[]{:S(2)}, u32[]{:S(2)}) async-start(bf16[32,8,1,2,4096]{4,3,0,2,1:T(2,128)(2,1)} %copy.188), calls=%async_computation.7 | async-start | bytes 8388608 | tf_op jit(solution)/shard_map/all_to_all | solution.py:184
  495.5 8.8 %copy-start.1 = (bf16[384,4096]{1,0:T(8,128)(2,1)S(1)}, bf16[384,4096]{1,0:T(8,128)(2,1)}, u32[]{:S(2)}) copy-start(bf16[384,4096]{1,0:T(8,128)(2,1)} %param.21) | copy-start | bytes 9437188
where the time goes:
time: 513 us; the launch traced here: 505 us
  waiting for transfers between devices  219 us (43%)
  blocking collectives  102 us (20%)
  local copies, waits for them, and re-layouts  78.7 us (15%)
  starting transfers between devices  52.7 us (10%)
  other arithmetic  34.8 us (7%)
  matrix products  16.7 us (3%)
    all_to_all x1, blocking collectives, local(): lax.all_to_all(partial_value.astype(jnp.bfloat16), 'inst', split_axis=0,...  102 us
    all_to_all x1, waiting for transfers between devices, local(): lax.all_to_all(outgoing, 'inst', split_axis=0, concat_axis=0, tiled=True)  86.2 us
    all_to_all x1, waiting for transfers between devices, local(): lax.all_to_all(lax.all_to_all(outgoing, 'inst', split_axis=0, concat_axis...  39.5 us
    all_to_all x1, waiting for transfers between devices, local(): lax.all_to_all(lax.all_to_all(partial_value.astype(jnp.bfloat16), 'inst',...  39.1 us
    all_to_all x1, waiting for transfers between devices, local(): lax.all_to_all(packed_cache, 'inst', split_axis=0, concat_axis=0, tiled=T...  34.6 us
    all_to_all x1, waiting for transfers between devices, local(): lax.all_to_all(lax.all_to_all(packed_cache, 'inst', split_axis=0, concat_...  19.4 us
    all_to_all x1, starting transfers between devices, local(): lax.all_to_all(packed_tokens, 'inst', split_axis=0, concat_axis=0, tiled=...  11.6 us
    convert_element_type x2, local copies, waits for them, and re-layouts, local(): expert_out.reshape(expert_count * expert_cap, model_width)  11.5 us
  transfers between devices with their start and end apart: 7, of which 5 were waited for; matrix products, arithmetic and copies ran while one was open for 17% of the time, Pallas kernels for 0%

commit v1 on v0

v1 whole, which is shorter than its diff:
```python
import functools

import jax
import jax.numpy as jnp
from jax import lax
from jax.experimental import pallas as pl
from jax.experimental.pallas import tpu as pltpu
from jax.sharding import PartitionSpec as P

MESH = pl.DeviceIdType.MESH
F32 = jnp.float32
BF16 = jnp.bfloat16

D = 4096
UNITS = 384
NCH = 4
DC = D // NCH
TOK = 16
NZ = 8
COL = TOK * NZ
NR = 32
ROWS = NR * TOK
PROMPTS = 24
KVB = 144

STEPS = [
    (1, 0), (3, 0), (0, 1), (0, 3), (1, 1), (3, 3), (1, 3), (3, 1),
    (2, 0), (0, 2), (2, 1), (1, 2), (2, 3), (3, 2), (2, 2),
]
PLANE = [(0, 0, 1)] + [(a, b, 0) for a, b in STEPS] + [(a, b, 1) for a, b in STEPS]
ZSTEPS = (1, 7, 2, 6, 3, 5, 4)


def place():
    i, h = lax.axis_index("inst"), lax.axis_index("head")
    return i // 8, h // 2, lax.rem(i, 8) // 2, lax.rem(h, 2), lax.rem(i, 2)


def device(x, y, z_hi, z_lo, core):
    return (x * 8 + z_hi * 2 + core, y * 2 + z_lo)


def in_plane(dx, dy, dc):
    x, y, zh, zl, c = place()
    return device(lax.rem(x + dx + 4, 4), lax.rem(y + dy + 4, 4), zh, zl, lax.rem(c + dc, 2))


def along_z(dz):
    x, y, zh, zl, c = place()
    z = lax.rem(zh * 2 + zl + dz + 8, 8)
    return device(x, y, z // 2, lax.rem(z, 2), c)


def remote(src, dst, send, recv, dev):
    return pltpu.make_async_remote_copy(
        src_ref=src, dst_ref=dst, send_sem=send, recv_sem=recv, device_id=dev, device_id_type=MESH
    )


def drain(ref, sem):
    pltpu.make_async_copy(ref, ref, sem).wait()


def nt(a, b):
    return lax.dot_general(a, b, (((1,), (1,)), ((), ())), preferred_element_type=F32)


def kernel(
    rows_sm, lens_sm, slot_sm, route, tok, kv, qf, wg_hbm, wu_hbm, wd_hbm,
    hand_hbm, att, moe,
    rbuf, gtok, sel, xin, pout, rin, comb, zin, wg, wu, wd, gacc, uacc, pick, mix,
    kvs, kvr, hand,
    id_s, id_r, zs, zr, xs, xr, rs, rr, cs, cr, ws, ks, ks0, kr, hs,
):
    inst, head = lax.axis_index("inst"), lax.axis_index("head")
    x, y, zh, zl, core = place()
    z = zh * 2 + zl

    barrier = pltpu.get_barrier_semaphore()
    for dx, dy, dc in PLANE:
        pl.semaphore_signal(barrier, inc=1, device_id=in_plane(-dx, -dy, dc), device_id_type=MESH)
    for dz in ZSTEPS:
        pl.semaphore_signal(barrier, inc=1, device_id=along_z(dz), device_id_type=MESH)

    @pl.loop(0, 32)
    def _(t):
        src_i, src_h = head * 4 + t // 8, lax.rem(t, 8)

        @pl.when(jnp.logical_or(src_i != inst, src_h != head))
        def _():
            pl.semaphore_signal(barrier, inc=1, device_id=(src_i, src_h), device_id_type=MESH)

    def weight_copies():
        for n, (src, dst) in enumerate(((wg_hbm, wg), (wu_hbm, wu), (wd_hbm, wd))):
            for c in range(NCH):
                yield pltpu.make_async_copy(src.at[:, pl.ds(c * DC, DC)], dst.at[c], ws.at[n * NCH + c])

    kv_head = inst // 4
    self_kv = kv_head == head
    pl.semaphore_wait(barrier, 31 + 7 + 32 - self_kv.astype(jnp.int32))

    zrows = pl.ds(pl.multiple_of(z * TOK, TOK), TOK)
    pltpu.make_async_copy(route, rbuf.at[z], id_r).start()
    for dz in ZSTEPS:
        remote(route, rbuf.at[z], id_s, id_r, along_z(dz)).start()

    @pl.loop(0, NCH)
    def _(c):
        piece = tok.at[:, pl.ds(pl.multiple_of(c * DC, DC), DC)]
        pltpu.make_async_copy(piece, gtok.at[c, zrows, :], zr.at[c]).start()
        for dz in ZSTEPS:
            remote(piece, gtok.at[c, zrows, :], zs.at[c], zr.at[c], along_z(dz)).start()

    for copy in weight_copies():
        copy.start()

    @pl.loop(0, 64)
    def _(t):
        row, live = rows_sm[t], lens_sm[t]
        mask = lax.broadcasted_iota(jnp.int32, (128, 128), 1) < live
        block = kv[row]
        kvs[t // 2, lax.rem(t, 2), 0:128, :] = jnp.where(mask, block, jnp.zeros_like(block))
        line = qf[row]
        kvs[t // 2, lax.rem(t, 2), 128:144, :] = jnp.where(
            jnp.broadcast_to(live > 0, (16, 128)), line, jnp.zeros_like(line)
        )

    drain(rbuf, id_r)
    routes = jnp.sum(rbuf[...], axis=0)
    r = lax.broadcasted_iota(jnp.int32, (NR, COL), 0)
    ex, ey, ec = lax.rem(x + r // 8, 4), lax.rem(y + lax.rem(r // 2, 4), 4), lax.rem(core + r, 2)
    expert = ((ex * 8 + zh * 2 + ec) * 4 + ey).astype(F32)
    match = jnp.zeros((NR, COL), F32)
    gate = jnp.zeros((NR, COL), F32)
    for k in range(8):
        hit = routes[k : k + 1, :] == expert
        match = match + jnp.where(hit, 1.0, 0.0)
        gate = gate + jnp.where(hit, routes[8 + k : 9 + k, :], 0.0)
    a = lax.broadcasted_iota(jnp.int32, (COL, COL), 0)
    b = lax.broadcasted_iota(jnp.int32, (COL, COL), 1)
    before = jnp.where((a // TOK == b // TOK) & (a < b), 1.0, 0.0).astype(BF16)
    rank = jnp.dot(match.astype(BF16), before, preferred_element_type=F32)
    key = jnp.where(match > 0.0, rank, -1.0)
    wide = lambda v: jnp.broadcast_to(v[:, None, :], (NR, TOK, COL)).reshape(ROWS, COL)
    row = lax.rem(lax.broadcasted_iota(jnp.int32, (ROWS, COL), 0), TOK)
    lane = lax.broadcasted_iota(jnp.int32, (ROWS, COL), 1)
    chosen = (wide(key) == lax.rem(row, 2).astype(F32)) & (lane // TOK == row // 2)
    pick[...] = jnp.where(chosen, 1.0, 0.0).astype(BF16)
    mix[...] = jnp.transpose(jnp.where(chosen, wide(gate), 0.0)).astype(BF16)

    @pl.loop(0, NCH)
    def _(c):
        drain(gtok.at[c], zr.at[c])
        sel[c] = jnp.dot(pick[...], gtok[c], preferred_element_type=F32).astype(BF16)
        pltpu.make_async_copy(sel.at[c, pl.ds(0, TOK)], xin.at[c, pl.ds(0, TOK)], xr.at[c]).start()
        for dx, dy, dc in PLANE:
            block = pl.ds((dx * 8 + dy * 2 + dc) * TOK, TOK)
            remote(sel.at[c, block], xin.at[c, block], xs.at[c], xr.at[c], in_plane(dx, dy, dc)).start()

    mine = lax.rem(inst, 4) * 8 + head

    @pl.when(self_kv)
    def _():
        pltpu.make_async_copy(kvs.at[inst], kvr.at[mine], kr).start()

    @pl.when(jnp.logical_not(self_kv))
    def _():
        remote(kvs.at[inst], kvr.at[mine], ks0, kr, (inst, kv_head)).start()

    @pl.loop(1, 32)
    def _(t):
        dest = lax.rem(x + t // 8, 4) * 8 + lax.rem(zh + lax.rem(t // 2, 4), 4) * 2 + lax.rem(core + t, 2)
        remote(kvs.at[dest], kvr.at[mine], ks, kr, (dest, kv_head)).start()

    for copy in weight_copies():
        copy.wait()
    gacc[...] = jnp.zeros_like(gacc)
    uacc[...] = jnp.zeros_like(uacc)

    @pl.loop(0, NCH)
    def _(c):
        drain(xin.at[c], xr.at[c])
        gacc[...] += nt(xin[c], wg[c])
        uacc[...] += nt(xin[c], wu[c])

    hidden = (gacc[...] / (1.0 + jnp.exp(-gacc[...])) * uacc[...]).astype(BF16)

    @pl.loop(0, NCH)
    def _(c):
        pout[c] = jnp.dot(hidden, wd[c], preferred_element_type=F32).astype(BF16)
        pltpu.make_async_copy(pout.at[c, pl.ds(0, TOK)], rin.at[c, pl.ds(0, TOK)], rr.at[c]).start()
        for dx, dy, dc in PLANE:
            block = pl.ds((dx * 8 + dy * 2 + dc) * TOK, TOK)
            remote(pout.at[c, block], rin.at[c, block], rs.at[c], rr.at[c], in_plane(-dx, -dy, dc)).start()

    drain(kvr, kr)
    a = lax.broadcasted_iota(jnp.int32, (128, 128), 0)
    b = lax.broadcasted_iota(jnp.int32, (128, 128), 1)
    eye = jnp.where(a == b, 1.0, 0.0).astype(BF16)

    @pl.loop(0, 8)
    def _(i):
        s, c = i // 2, lax.rem(i, 2)
        keys = jnp.concatenate([kvr[s * 8 + h, c, 0:64, :] for h in range(8)], axis=0)
        values = jnp.concatenate([kvr[s * 8 + h, c, 64:128, :] for h in range(8)], axis=0)
        lines = [kvr[s * 8 + h, c, 128:144, :].astype(F32) for h in range(8)]
        hand[i, 0] = nt(eye, keys).astype(BF16)
        hand[i, 1] = nt(eye, values).astype(BF16)
        live = lax.broadcasted_iota(jnp.int32, (16, 128), 1) < slot_sm[i]
        for k in range(4):
            q = jnp.concatenate([lines[2 * k][0:8], lines[2 * k + 1][0:8]], axis=0)
            score = jnp.dot(q.astype(BF16), keys[k * 128 : (k + 1) * 128], preferred_element_type=F32) * 128**-0.5
            own = jnp.sum(q * lines[k][8:9], axis=1, keepdims=True) * 128**-0.5
            top = jnp.maximum(jnp.max(jnp.where(live, score, -1e30), axis=1, keepdims=True), own)
            e = jnp.where(live, jnp.exp(score - top), 0.0)
            eo = jnp.exp(own - top)
            total = jnp.sum(e, axis=1, keepdims=True) + eo
            w = (e / total).astype(BF16)
            wo = (eo / total).astype(BF16).astype(F32)
            o = nt(w, values[k * 128 : (k + 1) * 128]) + wo * lines[4 + k][8:9]
            att[i, k * 16 : (k + 1) * 16, :] = o.astype(BF16)

    pltpu.make_async_copy(hand, hand_hbm, hs).start()

    @pl.loop(0, NCH)
    def _(c):
        drain(rin.at[c], rr.at[c])
        comb[c] = jnp.dot(mix[...], rin[c], preferred_element_type=F32).astype(BF16)
        pltpu.make_async_copy(comb.at[c, zrows], zin.at[c, z], cr.at[c]).start()
        for dz in ZSTEPS:
            there = pl.ds(pl.multiple_of(lax.rem(z + dz, 8) * TOK, TOK), TOK)
            remote(comb.at[c, there], zin.at[c, z], cs.at[c], cr.at[c], along_z(dz)).start()

    @pl.loop(0, NCH)
    def _(c):
        drain(zin.at[c], cr.at[c])
        moe[:, pl.ds(pl.multiple_of(c * DC, DC), DC)] = jnp.sum(zin[c].astype(F32), axis=0).astype(BF16)

    drain(rbuf.at[pl.ds(0, 7)], id_s)
    drain(kvs.at[pl.ds(0, 31)], ks)

    @pl.when(jnp.logical_not(self_kv))
    def _():
        drain(kvs.at[0], ks0)

    @pl.loop(0, NCH)
    def _(c):
        drain(gtok.at[c, pl.ds(0, 7 * TOK)], zs.at[c])
        drain(sel.at[c, pl.ds(0, 31 * TOK)], xs.at[c])
        drain(pout.at[c, pl.ds(0, 31 * TOK)], rs.at[c])
        drain(comb.at[c, pl.ds(0, 7 * TOK)], cs.at[c])

    pltpu.make_async_copy(hand, hand_hbm, hs).wait()


def slots(owners, lengths, target):
    p = jnp.arange(PROMPTS, dtype=jnp.int32)
    same = (owners[..., :, None] == owners[..., None, :]) & (p[None, :] < p[:, None])
    rank = jnp.sum(same.astype(jnp.int32), axis=-1)
    hit = (owners[..., None, None, :] == target[..., :, None, None]) & (
        rank[..., None, None, :] == jnp.arange(2, dtype=jnp.int32)[:, None]
    )
    rows = jnp.sum(jnp.where(hit, p, 0), axis=-1)
    lens = jnp.sum(jnp.where(hit, lengths[..., None, None, :], 0), axis=-1)
    return rows, lens


def local(kv_cache, query, fresh_kv, lengths, owner, tokens, expert_ids, gate_weights, w_gate, w_up, w_down):
    inst, head = lax.axis_index("inst"), lax.axis_index("head")
    owners, lens = owner[:, 0].reshape(32, PROMPTS), lengths.reshape(32, PROMPTS)
    own_o = lax.dynamic_index_in_dim(owners, inst, 0, keepdims=False)
    own_l = lax.dynamic_index_in_dim(lens, inst, 0, keepdims=False)
    send_rows, send_lens = slots(own_o, own_l, jnp.arange(32, dtype=jnp.int32))
    src_o = lax.dynamic_slice_in_dim(owners, head * 4, 4, 0)
    src_l = lax.dynamic_slice_in_dim(lens, head * 4, 4, 0)
    _, slot_lens = slots(src_o, src_l, jnp.broadcast_to(inst, (4, 1)))

    z = lax.rem(inst, 8) // 2 * 2 + lax.rem(head, 2)
    route = jnp.concatenate([expert_ids.T.astype(F32), gate_weights.T], axis=0)
    lane = jnp.arange(COL, dtype=jnp.int32)
    route = jnp.where(lane[None, :] // TOK == z, jnp.tile(route, (1, NZ)), 0.0)

    kv = jnp.swapaxes(kv_cache, 2, 3).reshape(PROMPTS, 128, 128)
    qf = jnp.concatenate([query.reshape(PROMPTS, 8, 128), fresh_kv[:, None, :]], axis=1)
    qf = jnp.pad(qf, ((0, 0), (0, 7), (0, 0)))

    vmem, smem, hbm = (pl.BlockSpec(memory_space=s) for s in (pltpu.VMEM, pltpu.SMEM, pl.ANY))
    dma = pltpu.SemaphoreType.DMA
    handed, att, moe = pl.pallas_call(
        kernel,
        out_shape=(
            jax.ShapeDtypeStruct((8, 2, 128, 512), BF16),
            jax.ShapeDtypeStruct((8, 64, 128), BF16),
            jax.ShapeDtypeStruct((TOK, D), BF16),
        ),
        in_specs=[smem] * 3 + [vmem] * 4 + [hbm] * 3,
        out_specs=(hbm, vmem, vmem),
        scratch_shapes=[
            pltpu.VMEM((NZ, 16, COL), F32),
            pltpu.VMEM((NCH, COL, DC), BF16),
            pltpu.VMEM((NCH, ROWS, DC), BF16),
            pltpu.VMEM((NCH, ROWS, DC), BF16),
            pltpu.VMEM((NCH, ROWS, DC), BF16),
            pltpu.VMEM((NCH, ROWS, DC), BF16),
            pltpu.VMEM((NCH, COL, DC), BF16),
            pltpu.VMEM((NCH, NZ, TOK, DC), BF16),
            pltpu.VMEM((NCH, UNITS, DC), BF16),
            pltpu.VMEM((NCH, UNITS, DC), BF16),
            pltpu.VMEM((NCH, UNITS, DC), BF16),
            pltpu.VMEM((ROWS, UNITS), F32),
            pltpu.VMEM((ROWS, UNITS), F32),
            pltpu.VMEM((ROWS, COL), BF16),
            pltpu.VMEM((COL, ROWS), BF16),
            pltpu.VMEM((32, 2, KVB, 128), BF16),
            pltpu.VMEM((32, 2, KVB, 128), BF16),
            pltpu.VMEM((8, 2, 128, 512), BF16),
            dma, dma, dma((NCH,)), dma((NCH,)), dma((NCH,)), dma((NCH,)), dma((NCH,)), dma((NCH,)),
            dma((NCH,)), dma((NCH,)), dma((3 * NCH,)), dma, dma, dma, dma,
        ],
        compiler_params=pltpu.CompilerParams(
            collective_id=1, has_side_effects=True, vmem_limit_bytes=58 * 2**20
        ),
    )(
        send_rows.reshape(64), send_lens.reshape(64), slot_lens.reshape(8), route, tokens, kv, qf,
        w_gate, w_up, w_down,
    )
    return handed, att.reshape(8, 8192), moe


def solution(mesh):
    both = P(("inst", "head"), None)
    in_specs = (
        P("inst", None, None, "head"), P("inst", "head"), P("inst", "head"), P(), P(),
        both, both, both, both, both, both,
    )
    out_specs = (P(("inst", "head"), None, None, None), both, both)
    return jax.shard_map(local, mesh=mesh, in_specs=in_specs, out_specs=out_specs, check_vma=False)
```

time: 513 us -> 198 us (0.39); the launches traced: 505 us -> 195 us
  waiting for transfers between devices: 219 us -> 0 us
  Pallas kernels: 0 us -> 180 us
  blocking collectives: 102 us -> 0 us
  local copies, waits for them, and re-layouts: 78.7 us -> 10 us
  starting transfers between devices: 52.7 us -> 0 us
  other arithmetic: 34.8 us -> 4.1 us
  matrix products: 16.7 us -> 0 us
    all_to_all x7 -> x0, waiting for transfers between devices: 219 us -> none  [the longest x1 86.2 us: local(): lax.all_to_all(outgoing, 'inst', split_axis=0, concat_axis=0, tiled=True)]
    pallas_call x0 -> x1, Pallas kernels: none -> 180 us  [local(): pl.pallas_call(kernel, out_shape=(jax.ShapeDtypeStruct((8, 2, 128, 512),...]
    all_to_all x1 -> x0, blocking collectives: 102 us -> none  [local(): lax.all_to_all(partial_value.astype(jnp.bfloat16), 'inst', split_axis=0,...]
    all_to_all x7 -> x0, starting transfers between devices: 52.7 us -> none  [the longest x1 11.6 us: local(): lax.all_to_all(packed_tokens, 'inst', split_axis=0, concat_axis=0, tiled=...]
    all_to_all x3 -> x0, local copies, waits for them, and re-layouts: 18.8 us -> none  [the longest x1 8.5 us: local(): lax.all_to_all(outgoing, 'inst', split_axis=0, concat_axis=0, tiled=True)]
    gather x8 -> x0, local copies, waits for them, and re-layouts: 18.3 us -> none  [the longest x2 7.56 us: local(): jnp.take(tokens, pick_rows.reshape(-1), axis=0)]
    dot_general x6 -> x0, matrix products: 16.7 us -> none  [the longest x1 6.03 us: local(): jnp.einsum('ihecd,eud->ihecu', incoming, gate_rows, preferred_element_typ...]
    reduce_sum x8 -> x4, other arithmetic: 13.6 us -> 0.63 us  [the longest x2 0.39 us: slots(): rank = jnp.sum(same.astype(jnp.int32), axis=-1)]
  transfers between devices with their start and end apart: 7 -> 0, of which waited for: 5 -> 0; matrix products, arithmetic and copies ran while one was open for 17% -> 0% of each run, Pallas kernels for 0% -> 0%
where the time goes in v1:
time: 198 us; the launch traced here: 195 us
  Pallas kernels  180 us (91%)
  local copies, waits for them, and re-layouts  10 us (5%)
  other arithmetic  4.1 us (2%)
    pallas_call x1, Pallas kernels, local(): pl.pallas_call(kernel, out_shape=(jax.ShapeDtypeStruct((8, 2, 128, 512),...  180 us
    unnamed x6, local copies, waits for them, and re-layouts  6.24 us

profile of v1, /device:TPU:2, one launch (start us, length us, event | category | flops | bytes accessed | tf_op | source)
XLA Modules:
  0.0 195.0 jit_solution(7723229111799566932)
XLA Ops:
  0.7 0.7 reduce.1
  1.4 0.7 convert_bitcast_fusion
  2.1 0.7 pad_maximum_fusion
  2.8 0.1 reshape_squeeze.3
  2.9 0.2 convert_reduce_fusion
  3.1 0.7 copy.18
  3.8 0.8 reshape.166
  4.6 0.1 select_reduce_fusion
  4.8 0.2 convert_reduce_fusion.1
  5.0 0.1 copy.17
  5.1 0.6 reshape.168.slot_sm
  5.7 0.1 iota_compare_fusion.2
  5.7 0.1 fusion.4
  5.8 0.1 copy.16
  5.9 0.6 reshape.167.lens_sm
  6.5 0.1 copy.15
  6.6 0.6 reshape.165.rows_sm
  7.3 0.8 copy.19
  8.1 0.7 fusion.2.qf
  8.7 0.1 tile.10
  8.8 0.6 broadcast_select_fusion.route
  9.4 180.1 %shard_map.130 = (bf16[8,2,128,512]{3,2,1,0:T(8,128)(2,1)}, bf16[8,64,128]{2,1,0:T(8,128)(2,1)}, bf16[16,4096]{1,0:T(8,128)(2,1)}) custom-call(s32[64]{0:T(128)} %reshape.165.rows_sm, s32[64]{0:T(128)} %reshape.167.lens_sm, s32[8]{0:T(128)} %reshape.168.slot_sm, f32[16,128]{1,0:T(8,128)} %broadcast_select_fusion.route, bf16[16,4096]{1,0:T(8,128)(2,1)} %tok.1, ...), custom_call_target="tpu_custom_call" | custom-call | tf_op jit(solution)/shard_map/pallas_call | solution.py:289
  189.5 0.0 copy-start
  189.5 1.7 copy.22
  191.2 3.1 %copy.25 = bf16[8,2,128,512]{3,2,1,0:T(8,128)(2,1)} copy(bf16[8,2,128,512]{3,2,1,0:T(8,128)(2,1)} %get-tuple-element.18) | data formatting | bytes 4194304
  194.3 0.0 copy-done
  194.3 0.7 copy.26
  (7 shorter events, 0.1 us)
Async XLA Ops:
  189.5 4.8 %copy-start = (bf16[16,4096]{1,0:T(8,128)(2,1)S(1)}, bf16[16,4096]{1,0:T(8,128)(2,1)}, u32[]{:S(2)}) copy-start(bf16[16,4096]{1,0:T(8,128)(2,1)} %get-tuple-element.20) | copy-start | bytes 393220

commit v2 on v1

v2 whole, which is shorter than its diff:
```python
import functools

import jax
import jax.numpy as jnp
from jax import lax
from jax.experimental import pallas as pl
from jax.experimental.pallas import tpu as pltpu
from jax.sharding import PartitionSpec as P

MESH = pl.DeviceIdType.MESH
F32 = jnp.float32
BF16 = jnp.bfloat16

D = 4096
UNITS = 384
NCH = 8
DC = D // NCH
NZP = 4
AHEAD = 4
BACK = 4
TURN_Y = (-1, 0)
TURN_Z = (1, 3)
REST = 9
TOK = 16
NZ = 8
COL = TOK * NZ
NR = 32
ROWS = NR * TOK
PROMPTS = 24
KVB = 144

SPREAD = ((0, 1), (1, 0), (3, 0), (2, 0), (1, 1), (3, 1), (2, 1))
PEERS = [(d, 0, c) for d in range(4) for c in range(2) if d + c] + [(0, d, c) for d in (1, 2, 3) for c in range(2)]
ZSTEPS = (1, 7, 2, 6, 3, 5, 4)


def place():
    i, h = lax.axis_index("inst"), lax.axis_index("head")
    return i // 8, h // 2, lax.rem(i, 8) // 2, lax.rem(h, 2), lax.rem(i, 2)


def device(x, y, z_hi, z_lo, core):
    return (x * 8 + z_hi * 2 + core, y * 2 + z_lo)


def in_plane(dx, dy, dc):
    x, y, zh, zl, c = place()
    return device(lax.rem(x + dx + 4, 4), lax.rem(y + dy + 4, 4), zh, zl, lax.rem(c + dc, 2))


def along_z(dz):
    x, y, zh, zl, c = place()
    z = lax.rem(zh * 2 + zl + dz + 8, 8)
    return device(x, y, z // 2, lax.rem(z, 2), c)


def remote(src, dst, send, recv, dev):
    return pltpu.make_async_remote_copy(
        src_ref=src, dst_ref=dst, send_sem=send, recv_sem=recv, device_id=dev, device_id_type=MESH
    )


def drain(ref, sem):
    pltpu.make_async_copy(ref, ref, sem).wait()


def nt(a, b):
    return lax.dot_general(a, b, (((1,), (1,)), ((), ())), preferred_element_type=F32)


def kernel(
    code_sm, route, tok, kv, qf, wg_hbm, wu_hbm, wd_hbm,
    hand_hbm, att, moe,
    rbuf, rcol, xg, sel, xin, pout, rin, pc, via, side, comb, zin, wg, wu, wd, gacc, uacc, pick, mix,
    kvs, kvm, kvy, kvr, hand, heads,
    id_s, id_r, rc_s, rc_r, zs, zr, ds, dr, fs, fr, xs, xr, rs, rr, vs, vr, ss, sr, cs, cr, ws, ks, ks0, kr, ms, mr, ys, yr, hs,
):
    inst, head = lax.axis_index("inst"), lax.axis_index("head")
    x, y, zh, zl, core = place()
    z = zh * 2 + zl

    barrier = pltpu.get_barrier_semaphore()
    for dx, dy, dc in PEERS:
        pl.semaphore_signal(barrier, inc=1, device_id=in_plane(-dx, -dy, dc), device_id_type=MESH)
    for dz in ZSTEPS:
        pl.semaphore_signal(barrier, inc=1, device_id=along_z(dz), device_id_type=MESH)

    for t in range(8):
        src_z = zl * 4 + t // 2
        src_i, src_h = x * 8 + src_z // 2 * 2 + t % 2, y * 2 + lax.rem(src_z, 2)

        @pl.when(jnp.logical_or(src_i != inst, src_h != head))
        def _():
            pl.semaphore_signal(barrier, inc=1, device_id=(src_i, src_h), device_id_type=MESH)

    def weight_copies():
        for n, (src, dst) in enumerate(((wg_hbm, wg), (wu_hbm, wu), (wd_hbm, wd))):
            for c in range(NCH):
                yield pltpu.make_async_copy(src.at[:, pl.ds(c * DC, DC)], dst.at[c], ws.at[n * NCH + c])

    def dense(c, d):
        return in_plane(d, 0, 0) if c % 2 == 0 else in_plane(0, d, 0)

    def spread(c, d, dc):
        return in_plane(0, d, dc) if c % 2 == 0 else in_plane(d, 0, dc)

    def rows_of(ref, c, d, dc):
        return ref.at[c, :, d, dc] if c % 2 == 0 else ref.at[c, d, :, dc]

    near, far = lambda c: (1, 3) if c // 2 % 2 == 0 else (3, 1), 2
    self_kv = zl == zh // 2
    pl.semaphore_wait(barrier, 13 + 7 + 8 - self_kv.astype(jnp.int32))

    zrows = lambda h: pl.ds(pl.multiple_of(lax.rem(z + h + 8, 8) * TOK, TOK), TOK)
    pltpu.make_async_copy(route, rbuf.at[z], id_r).start()
    for dz in ZSTEPS:
        remote(route, rbuf.at[z], id_s, id_r, along_z(dz)).start()
    hops = lambda p: (4, 3) if p % 2 == 0 else (3, 4)
    up, down = along_z(1), along_z(-1)

    def z_block(p, way, h):
        return xg.at[pl.ds(2 * p, 2), 0, zrows(-h if way == 0 else h), :]

    def z_copy(p, way, h):
        block = z_block(p, way, h)
        return remote(block, block, zs.at[p], zr.at[p, way * 4 + h], up if way == 0 else down)

    def z_wait(p, way, h):
        drain(z_block(p, way, h), zr.at[p, way * 4 + h - 1])

    for p in range(NZP):
        for c in (2 * p, 2 * p + 1):
            xg[c, 0, zrows(0), :] = tok[:, c * DC : (c + 1) * DC]
        z_copy(p, 0, 0).start()
        z_copy(p, 1, 0).start()

    for copy in weight_copies():
        copy.start()

    def pack(n):
        @pl.loop(0, 32)
        def _(t):
            code = code_sm[t * 2 + n]
            row, live = code // 256, lax.rem(code, 256)
            mask = lax.broadcasted_iota(jnp.int32, (128, 128), 1) < live
            block = kv[row]
            kvs[n, t, 0:128, :] = jnp.where(mask, block, jnp.zeros_like(block))
            line = qf[row]
            kvs[n, t, 128:144, :] = jnp.where(
                jnp.broadcast_to(live > 0, (16, 128)), line, jnp.zeros_like(line)
            )

        for d in (1, 3, 2):
            there = kvs.at[n, pl.ds(lax.rem(x + d, 4) * 8, 8)]
            remote(there, kvm.at[n, x], ms.at[n], mr.at[n], in_plane(d, 0, 0)).start()
        pltpu.make_async_copy(kvs.at[n, pl.ds(x * 8, 8)], kvm.at[n, x], mr.at[n]).start()

    pack(0)
    for h in (1, 2, 3):
        for p in range(NZP):
            for way in (0, 1):
                z_wait(p, way, h)
                if h < hops(p)[way]:
                    z_copy(p, way, h).start()
        if h == 1:
            pack(1)
        if h == 1:
            drain(rbuf, id_r)
            routes = jnp.sum(rbuf[...], axis=0)
            rcol[0, 0] = routes
            rcol[1, 0] = routes
            for d in (1, 2, 3):
                remote(rcol.at[0, 0], rcol.at[0, d], rc_s.at[0], rc_r.at[0], in_plane(d, 0, 0)).start()
                remote(rcol.at[1, 0], rcol.at[1, d], rc_s.at[1], rc_r.at[1], in_plane(0, d, 0)).start()

    def whole(c):
        if c % 2 == 0:
            z_wait(c // 2, c // 2 % 2, 4)
        for d in near(c):
            remote(xg.at[c, 0], xg.at[c, d], ds.at[c], dr.at[c, d], dense(c, d)).start()

    for c in range(AHEAD):
        whole(c)

    a = lax.broadcasted_iota(jnp.int32, (COL, COL), 0)
    b = lax.broadcasted_iota(jnp.int32, (COL, COL), 1)
    before = jnp.where((a // TOK == b // TOK) & (a < b), 1.0, 0.0).astype(BF16)
    r = lax.rem(lax.broadcasted_iota(jnp.int32, (NR, COL), 0), 8)
    row = lax.rem(lax.broadcasted_iota(jnp.int32, (ROWS, COL), 0), TOK)
    lane = lax.broadcasted_iota(jnp.int32, (ROWS, COL), 1)
    wide = lambda v: jnp.broadcast_to(v[:, None, :], (NR, TOK, COL)).reshape(ROWS, COL)
    for ty in range(2):
        drain(rcol.at[ty, pl.ds(0, 3)], rc_r.at[ty])
        ex = x if ty == 0 else lax.rem(x + r // 2, 4)
        ey = lax.rem(y + r // 2, 4) if ty == 0 else y
        expert = ((ex * 8 + zh * 2 + lax.rem(core + r, 2)) * 4 + ey).astype(F32)
        match = jnp.zeros((NR, COL), F32)
        gate = jnp.zeros((NR, COL), F32)
        for k in range(8):
            line = lambda n: jnp.concatenate(
                [jnp.broadcast_to(rcol[ty, d, n : n + 1, :], (8, COL)) for d in range(4)], axis=0
            )
            hit = line(k) == expert
            match = match + jnp.where(hit, 1.0, 0.0)
            gate = gate + jnp.where(hit, line(8 + k), 0.0)
        rank = jnp.dot(match.astype(BF16), before, preferred_element_type=F32)
        key = jnp.where(match > 0.0, rank, -1.0)
        chosen = (wide(key) == lax.rem(row, 2).astype(F32)) & (lane // TOK == row // 2)
        pick[ty] = jnp.where(chosen, 1.0, 0.0).astype(BF16)
        mix[ty] = jnp.transpose(jnp.where(chosen, wide(gate), 0.0)).astype(BF16)

    def along_y(n):
        drain(kvm.at[n], mr.at[n])
        for d in (1, 3, 2):
            there = kvm.at[n, lax.rem(y + d, 4)]
            remote(there, kvy.at[n, y], ys.at[n], yr.at[n], in_plane(0, d, 0)).start()
        pltpu.make_async_copy(kvm.at[n, y], kvy.at[n, y], yr.at[n]).start()

    def to_owner(n):
        drain(kvy.at[n], yr.at[n])
        mine = kvr.at[n, lax.rem(inst, 4), :, zl]

        def send(t, sem):
            to = lax.rem(zh + t // 2, 4) * 2 + lax.rem(core + t, 2)
            return remote(kvy.at[n, :, to], mine, sem, kr.at[n], (x * 8 + to, y * 2 + zh // 2))

        @pl.when(self_kv)
        def _():
            pltpu.make_async_copy(kvy.at[n, :, zh * 2 + core], mine, kr.at[n]).start()

        @pl.when(jnp.logical_not(self_kv))
        def _():
            send(0, ks0.at[n]).start()

        for t in range(1, 8):
            send(t, ks.at[n]).start()

    for n in range(2):
        if TURN_Y[n] < 0:
            along_y(n)

    def relay(c):
        first, second = near(c)
        drain(xg.at[c, first], dr.at[c, first])
        remote(xg.at[c, first], xg.at[c, far], fs.at[c], fr.at[c], dense(c, first)).start()

    def choose(c):
        first, second = near(c)
        for d in (0, first, second, far):
            if d == second:
                drain(xg.at[c, d], dr.at[c, d])
            if d == far:
                drain(xg.at[c, d], fr.at[c])
            rows = jnp.dot(pick[c % 2, d * 128 : (d + 1) * 128], xg[c, d], preferred_element_type=F32)
            sel[c, d] = rows.astype(BF16).reshape(4, 2, TOK, DC)
        pltpu.make_async_copy(sel.at[c, :, 0, 0], rows_of(xin, c, 0, 0), xr.at[c]).start()
        for d, dc in SPREAD:
            remote(sel.at[c, :, d, dc], rows_of(xin, c, d, dc), xs.at[c], xr.at[c], spread(c, d, dc)).start()

    for t in range(NCH + 1):
        if t < NCH:
            relay(t)
        if t + AHEAD < NCH:
            whole(t + AHEAD)
        if t >= 1:
            choose(t - 1)
        for n in range(2):
            if t == TURN_Y[n]:
                along_y(n)
            if t == TURN_Z[n]:
                to_owner(n)

    for copy in weight_copies():
        copy.wait()
    gacc[...] = jnp.zeros_like(gacc)
    uacc[...] = jnp.zeros_like(uacc)

    @pl.loop(0, NCH)
    def _(c):
        drain(xin.at[c], xr.at[c])
        rows = xin[c].reshape(ROWS, DC)
        gacc[...] += nt(rows, wg[c])
        uacc[...] += nt(rows, wu[c])

    hidden = (gacc[...] / (1.0 + jnp.exp(-gacc[...])) * uacc[...]).astype(BF16)

    def out(c):
        rows = jnp.dot(hidden, wd[c], preferred_element_type=F32)
        pout[c] = rows.astype(BF16).reshape(4, 4, 2, TOK, DC)
        pltpu.make_async_copy(rows_of(pout, c, 0, 0), rin.at[c, :, 0, 0], rr.at[c]).start()
        for d, dc in SPREAD:
            remote(rows_of(pout, c, d, dc), rin.at[c, :, d, dc], rs.at[c], rr.at[c], spread(c, -d, dc)).start()

    for c in range(BACK):
        out(c)

    def attend():
        drain(kvr.at[0], kr.at[0])
        drain(kvr.at[1], kr.at[1])
        a = lax.broadcasted_iota(jnp.int32, (128, 128), 0)
        b = lax.broadcasted_iota(jnp.int32, (128, 128), 1)
        eye = jnp.where(a == b, 1.0, 0.0).astype(BF16)

        @pl.loop(0, 8)
        def _(i):
            s, c = i // 2, lax.rem(i, 2)
            keys = jnp.concatenate([kvr[c, s, h // 2, h % 2, 0:64, :] for h in range(8)], axis=0)
            values = jnp.concatenate([kvr[c, s, h // 2, h % 2, 64:128, :] for h in range(8)], axis=0)
            lines = [kvr[c, s, h // 2, h % 2, 128:144, :].astype(F32) for h in range(8)]
            hand[i, 0] = nt(eye, keys).astype(BF16)
            hand[i, 1] = nt(eye, values).astype(BF16)
            live = lax.broadcasted_iota(jnp.int32, (16, 128), 1) < lax.rem(code_sm[64 + i], 256)
            for k in range(4):
                q = jnp.concatenate([lines[2 * k][0:8], lines[2 * k + 1][0:8]], axis=0)
                score = jnp.dot(q.astype(BF16), keys[k * 128 : (k + 1) * 128], preferred_element_type=F32) * 128**-0.5
                own = jnp.sum(q * lines[k][8:9], axis=1, keepdims=True) * 128**-0.5
                top = jnp.maximum(jnp.max(jnp.where(live, score, -1e30), axis=1, keepdims=True), own)
                e = jnp.where(live, jnp.exp(score - top), 0.0)
                eo = jnp.exp(own - top)
                total = jnp.sum(e, axis=1, keepdims=True) + eo
                w = (e / total).astype(BF16)
                wo = (eo / total).astype(BF16).astype(F32)
                o = nt(w, values[k * 128 : (k + 1) * 128]) + wo * lines[4 + k][8:9]
                heads[i, k * 16 : (k + 1) * 16, :] = o

        pltpu.make_async_copy(hand, hand_hbm, hs).start()

        for q in range(64):
            att[:, q * 128 : (q + 1) * 128] = heads[:, q, :].astype(BF16)

    def sums(c):
        drain(rin.at[c], rr.at[c])
        if c + BACK < NCH:
            out(c + BACK)
        first, second = near(c)
        for d in (far, second, first, 0):
            rows = rin[c, d].reshape(128, DC)
            pc[c, d] = jnp.dot(mix[c % 2, :, d * 128 : (d + 1) * 128], rows, preferred_element_type=F32).astype(BF16)
            if d == far:
                remote(pc.at[c, d], via.at[c], vs.at[c], vr.at[c], dense(c, -first)).start()
            if d == second:
                remote(pc.at[c, d], side.at[c, 1], ss.at[c, 1], sr.at[c, 1], dense(c, -d)).start()

    def passing(c):
        first, second = near(c)
        drain(via.at[c], vr.at[c])
        pc[c, first] = (pc[c, first].astype(F32) + via[c].astype(F32)).astype(BF16)
        remote(pc.at[c, first], side.at[c, 0], ss.at[c, 0], sr.at[c, 0], dense(c, -first)).start()

    def planes(c):
        drain(side.at[c, 1], sr.at[c, 1])
        drain(side.at[c, 0], sr.at[c, 0])
        total = pc[c, 0].astype(F32) + side[c, 0].astype(F32) + side[c, 1].astype(F32)
        comb[c] = total.astype(BF16)
        pltpu.make_async_copy(comb.at[c, zrows(0)], zin.at[c, z], cr.at[c]).start()
        for dz in ZSTEPS:
            remote(comb.at[c, zrows(dz)], zin.at[c, z], cs.at[c], cr.at[c], along_z(dz)).start()

    for t in range(NCH + 2):
        if t < NCH:
            sums(t)
        if 0 <= t - 1 < NCH:
            passing(t - 1)
        if 0 <= t - 2 < NCH:
            planes(t - 2)
        if t == REST:
            attend()

    for c in range(NCH):
        drain(zin.at[c], cr.at[c])
        moe[:, c * DC : (c + 1) * DC] = jnp.sum(zin[c].astype(F32), axis=0).astype(BF16)

    drain(rbuf.at[pl.ds(0, 7)], id_s)
    drain(rcol.at[0, pl.ds(0, 3)], rc_s.at[0])
    drain(rcol.at[1, pl.ds(0, 3)], rc_s.at[1])
    for n in range(2):
        drain(kvm.at[n, pl.ds(0, 3)], ms.at[n])
        drain(kvm.at[n, pl.ds(0, 3)], ys.at[n])
        drain(kvr.at[n, pl.ds(0, 3)], ks.at[n])
        drain(kvr.at[n, 0, pl.ds(0, 2)], ks.at[n])

        @pl.when(jnp.logical_not(self_kv))
        def _():
            drain(kvr.at[n, 0, pl.ds(0, 2)], ks0.at[n])

    for c in range(NCH):
        if c % 2 == 0:
            drain(xg.at[pl.ds(c, 2), 0, pl.ds(0, 7 * TOK)], zs.at[c // 2])
        drain(xg.at[c, pl.ds(0, 2)], ds.at[c])
        drain(xg.at[c, 0], fs.at[c])
        drain(xg.at[c, 0], vs.at[c])
        drain(xg.at[c, 0], ss.at[c, 0])
        drain(xg.at[c, 0], ss.at[c, 1])
        for ref, sem in ((sel, xs), (pout, rs)):
            drain(ref.at[c, pl.ds(0, 3)], sem.at[c])
            drain(ref.at[c, 3, pl.ds(0, 2)], sem.at[c])
        drain(comb.at[c, pl.ds(0, 7 * TOK)], cs.at[c])

    pltpu.make_async_copy(hand, hand_hbm, hs).wait()


def slots(owners, lengths, target):
    p = jnp.arange(PROMPTS, dtype=jnp.int32)
    same = (owners[..., :, None] == owners[..., None, :]) & (p[None, :] < p[:, None])
    rank = jnp.sum(same.astype(jnp.int32), axis=-1)
    hit = (owners[..., None, None, :] == target[..., :, None, None]) & (
        rank[..., None, None, :] == jnp.arange(2, dtype=jnp.int32)[:, None]
    )
    return jnp.sum(jnp.where(hit, (p * 256 + lengths)[..., None, None, :], 0), axis=-1)


def local(kv_cache, query, fresh_kv, lengths, owner, tokens, expert_ids, gate_weights, w_gate, w_up, w_down):
    inst, head = lax.axis_index("inst"), lax.axis_index("head")
    owners, lens = owner[:, 0].reshape(32, PROMPTS), lengths.reshape(32, PROMPTS)
    own_o = lax.dynamic_index_in_dim(owners, inst, 0, keepdims=False)
    own_l = lax.dynamic_index_in_dim(lens, inst, 0, keepdims=False)
    sends = slots(own_o, own_l, jnp.arange(32, dtype=jnp.int32))
    src_o = lax.dynamic_slice_in_dim(owners, head * 4, 4, 0)
    src_l = lax.dynamic_slice_in_dim(lens, head * 4, 4, 0)
    gets = slots(src_o, src_l, jnp.broadcast_to(inst, (4, 1)))
    codes = jnp.concatenate([sends.reshape(64), gets.reshape(8)])

    z = lax.rem(inst, 8) // 2 * 2 + lax.rem(head, 2)
    route = jnp.concatenate([expert_ids.T.astype(F32), gate_weights.T], axis=0)
    lane = jnp.arange(COL, dtype=jnp.int32)
    route = jnp.where(lane[None, :] // TOK == z, jnp.tile(route, (1, NZ)), 0.0)

    kv = jnp.swapaxes(kv_cache, 2, 3).reshape(PROMPTS, 128, 128)
    qf = jnp.concatenate([query.reshape(PROMPTS, 8, 128), fresh_kv[:, None, :]], axis=1)
    qf = jnp.pad(qf, ((0, 0), (0, 7), (0, 0)))

    vmem, smem, hbm = (pl.BlockSpec(memory_space=s) for s in (pltpu.VMEM, pltpu.SMEM, pl.ANY))
    dma = pltpu.SemaphoreType.DMA
    handed, att, moe = pl.pallas_call(
        kernel,
        out_shape=(
            jax.ShapeDtypeStruct((8, 2, 128, 512), BF16),
            jax.ShapeDtypeStruct((8, 64 * 128), BF16),
            jax.ShapeDtypeStruct((TOK, D), BF16),
        ),
        in_specs=[smem] + [vmem] * 4 + [hbm] * 3,
        out_specs=(hbm, vmem, vmem),
        scratch_shapes=[
            pltpu.VMEM((NZ, 16, COL), F32),
            pltpu.VMEM((2, 4, 16, COL), F32),
            pltpu.VMEM((NCH, 4, COL, DC), BF16),
            pltpu.VMEM((NCH, 4, 4, 2, TOK, DC), BF16),
            pltpu.VMEM((NCH, 4, 4, 2, TOK, DC), BF16),
            pltpu.VMEM((NCH, 4, 4, 2, TOK, DC), BF16),
            pltpu.VMEM((NCH, 4, 4, 2, TOK, DC), BF16),
            pltpu.VMEM((NCH, 4, COL, DC), BF16),
            pltpu.VMEM((NCH, COL, DC), BF16),
            pltpu.VMEM((NCH, 2, COL, DC), BF16),
            pltpu.VMEM((NCH, COL, DC), BF16),
            pltpu.VMEM((NCH, NZ, TOK, DC), BF16),
            pltpu.VMEM((NCH, UNITS, DC), BF16),
            pltpu.VMEM((NCH, UNITS, DC), BF16),
            pltpu.VMEM((NCH, UNITS, DC), BF16),
            pltpu.VMEM((ROWS, UNITS), F32),
            pltpu.VMEM((ROWS, UNITS), F32),
            pltpu.VMEM((2, ROWS, COL), BF16),
            pltpu.VMEM((2, COL, ROWS), BF16),
            pltpu.VMEM((2, 32, KVB, 128), BF16),
            pltpu.VMEM((2, 4, 8, KVB, 128), BF16),
            pltpu.VMEM((2, 4, 8, KVB, 128), BF16),
            pltpu.VMEM((2, 4, 4, 2, KVB, 128), BF16),
            pltpu.VMEM((8, 2, 128, 512), BF16),
            pltpu.VMEM((8, 64, 128), F32),
            dma, dma, dma((2,)), dma((2,)), dma((NZP,)), dma((NZP, 8)), dma((NCH,)), dma((NCH, 4)),
            dma((NCH,)), dma((NCH,)), dma((NCH,)), dma((NCH,)), dma((NCH,)), dma((NCH,)),
            dma((NCH,)), dma((NCH,)), dma((NCH, 2)), dma((NCH, 2)), dma((NCH,)), dma((NCH,)),
            dma((3 * NCH,)), dma((2,)), dma((2,)), dma((2,)), dma((2,)), dma((2,)), dma((2,)), dma((2,)), dma,
        ],
        compiler_params=pltpu.CompilerParams(
            collective_id=1, has_side_effects=True, vmem_limit_bytes=58 * 2**20
        ),
    )(
        codes, route, tokens, kv, qf,
        w_gate, w_up, w_down,
    )
    return handed, att, moe


def solution(mesh):
    both = P(("inst", "head"), None)
    in_specs = (
        P("inst", None, None, "head"), P("inst", "head"), P("inst", "head"), P(), P(),
        both, both, both, both, both, both,
    )
    out_specs = (P(("inst", "head"), None, None, None), both, both)
    return jax.shard_map(local, mesh=mesh, in_specs=in_specs, out_specs=out_specs, check_vma=False)
```

time: 198 us -> 183 us (0.924)
  Pallas kernels: 180 us -> 167 us
  local copies, waits for them, and re-layouts: 10 us -> 7.29 us
    pallas_call x1, Pallas kernels: 180 us -> 167 us  [local(): pl.pallas_call(kernel, out_shape=(jax.ShapeDtypeStruct((8, 2, 128, 512),...]
    unnamed x6 -> x8, local copies, waits for them, and re-layouts: 6.24 us -> 5.26 us
where the time goes in v2:
time: 183 us; the launch traced here: 179 us
  Pallas kernels  167 us (91%)
  local copies, waits for them, and re-layouts  7.29 us (4%)
  other arithmetic  4.73 us (3%)
    pallas_call x1, Pallas kernels, local(): pl.pallas_call(kernel, out_shape=(jax.ShapeDtypeStruct((8, 2, 128, 512),...  167 us
    unnamed x8, local copies, waits for them, and re-layouts  5.26 us

profile of v2, /device:TPU:2, one launch (start us, length us, event | category | flops | bytes accessed | tf_op | source)
XLA Modules:
  0.0 179.4 jit_solution(12838177777952463180)
XLA Ops:
  0.7 0.7 reduce.1
  1.4 0.7 convert_bitcast_fusion
  2.1 0.7 pad_maximum_fusion
  2.8 0.1 reshape_squeeze.3
  2.9 0.2 convert_reduce_fusion
  3.1 0.2 convert_reduce_fusion.1
  3.3 0.1 iota_compare_fusion.2
  3.4 0.7 copy.17
  4.1 0.8 reshape.170
  4.9 0.1 select_reduce_fusion.1
  5.1 0.1 select_reduce_fusion
  5.2 0.1 copy.16
  5.3 0.1 reshape.172
  5.3 0.1 copy.15
  5.4 0.1 reshape.171
  5.5 0.6 pad_add_fusion.code_sm
  6.1 0.8 copy.18
  6.9 0.7 fusion.2.qf
  7.6 0.1 tile.10
  7.7 0.6 broadcast_select_fusion.route
  8.3 166.6 %shard_map.130 = (bf16[8,2,128,512]{3,2,1,0:T(8,128)(2,1)}, bf16[8,8192]{1,0:T(8,128)(2,1)}, bf16[16,4096]{1,0:T(8,128)(2,1)}) custom-call(s32[72]{0:T(128)} %pad_add_fusion.code_sm, f32[16,128]{1,0:T(8,128)} %broadcast_select_fusion.route, bf16[16,4096]{1,0:T(8,128)(2,1)} %tok.1, bf16[24,128,128]{2,1,0:T(8,128)(2,1)} %bitcast.15, ...), custom_call_target="tpu_custom_call" | custom-call | tf_op jit(solution)/shard_map/pallas_call | solution.py:434
  174.9 0.0 copy-start.1
  174.9 0.0 copy-start
  174.9 3.1 %copy.22 = bf16[8,2,128,512]{3,2,1,0:T(8,128)(2,1)} copy(bf16[8,2,128,512]{3,2,1,0:T(8,128)(2,1)} %get-tuple-element.8) | data formatting | bytes 4194304
  178.0 0.0 copy-done.1
  178.0 0.7 copy.23
  178.7 0.0 copy-done
  178.7 0.7 copy.24
  (9 shorter events, 0.1 us)
Async XLA Ops:
  174.9 3.2 %copy-start.1 = (bf16[8,8192]{1,0:T(8,128)(2,1)S(1)}, bf16[8,8192]{1,0:T(8,128)(2,1)}, u32[]{:S(2)}) copy-start(bf16[8,8192]{1,0:T(8,128)(2,1)} %get-tuple-element.9) | copy-start | bytes 393220
  174.9 3.8 %copy-start = (bf16[16,4096]{1,0:T(8,128)(2,1)S(1)}, bf16[16,4096]{1,0:T(8,128)(2,1)}, u32[]{:S(2)}) copy-start(bf16[16,4096]{1,0:T(8,128)(2,1)} %get-tuple-element.10) | copy-start | bytes 393220

commit v3 on v2

--- a/solution.py
+++ b/solution.py
@@ -13,14 +13,15 @@
 
 D = 4096
 UNITS = 384
-NCH = 8
+NCH = 4
 DC = D // NCH
 NZP = 4
+PER = NCH // NZP
 AHEAD = 4
-BACK = 4
+BACK = 2
 TURN_Y = (-1, 0)
-TURN_Z = (1, 3)
-REST = 9
+TURN_Z = (1, 2)
+REST = 5
 TOK = 16
 NZ = 8
 COL = TOK * NZ
@@ -69,9 +70,9 @@
 
 
 def kernel(
-    code_sm, route, tok, kv, qf, wg_hbm, wu_hbm, wd_hbm,
+    code_sm, ids, gates, tok, kv, qf, wg_hbm, wu_hbm, wd_hbm,
     hand_hbm, att, moe,
-    rbuf, rcol, xg, sel, xin, pout, rin, pc, via, side, comb, zin, wg, wu, wd, gacc, uacc, pick, mix,
+    route, rbuf, rcol, xg, sel, xin, pout, rin, pc, via, side, comb, zin, wg, wu, wd, gacc, uacc, pick, mix,
     kvs, kvm, kvy, kvr, hand, heads,
     id_s, id_r, rc_s, rc_r, zs, zr, ds, dr, fs, fr, xs, xr, rs, rr, vs, vr, ss, sr, cs, cr, ws, ks, ks0, kr, ms, mr, ys, yr, hs,
 ):
@@ -79,6 +80,12 @@
     x, y, zh, zl, core = place()
     z = zh * 2 + zl
 
+    at = lax.broadcasted_iota(jnp.int32, (TOK, COL), 1) - lax.broadcasted_iota(jnp.int32, (TOK, COL), 0)
+    spots = jnp.where(at == z * TOK, 1.0, 0.0).astype(BF16)
+    for n, part in enumerate((ids, gates)):
+        part = part[...].astype(F32).astype(BF16)
+        route[n * 8 : (n + 1) * 8, :] = jnp.dot(part, spots, preferred_element_type=F32)
+
     barrier = pltpu.get_barrier_semaphore()
     for dx, dy, dc in PEERS:
         pl.semaphore_signal(barrier, inc=1, device_id=in_plane(-dx, -dy, dc), device_id_type=MESH)
@@ -119,7 +126,7 @@
     up, down = along_z(1), along_z(-1)
 
     def z_block(p, way, h):
-        return xg.at[pl.ds(2 * p, 2), 0, zrows(-h if way == 0 else h), :]
+        return xg.at[pl.ds(PER * p, PER), 0, zrows(-h if way == 0 else h), :]
 
     def z_copy(p, way, h):
         block = z_block(p, way, h)
@@ -129,7 +136,7 @@
         drain(z_block(p, way, h), zr.at[p, way * 4 + h - 1])
 
     for p in range(NZP):
-        for c in (2 * p, 2 * p + 1):
+        for c in range(PER * p, PER * p + PER):
             xg[c, 0, zrows(0), :] = tok[:, c * DC : (c + 1) * DC]
         z_copy(p, 0, 0).start()
         z_copy(p, 1, 0).start()
@@ -174,8 +181,8 @@
                 remote(rcol.at[1, 0], rcol.at[1, d], rc_s.at[1], rc_r.at[1], in_plane(0, d, 0)).start()
 
     def whole(c):
-        if c % 2 == 0:
-            z_wait(c // 2, c // 2 % 2, 4)
+        if c % PER == 0:
+            z_wait(c // PER, c // PER % 2, 4)
         for d in near(c):
             remote(xg.at[c, 0], xg.at[c, d], ds.at[c], dr.at[c, d], dense(c, d)).start()
 
@@ -384,8 +391,8 @@
             drain(kvr.at[n, 0, pl.ds(0, 2)], ks0.at[n])
 
     for c in range(NCH):
-        if c % 2 == 0:
-            drain(xg.at[pl.ds(c, 2), 0, pl.ds(0, 7 * TOK)], zs.at[c // 2])
+        if c % PER == 0:
+            drain(xg.at[pl.ds(c, PER), 0, pl.ds(0, 7 * TOK)], zs.at[c // PER])
         drain(xg.at[c, pl.ds(0, 2)], ds.at[c])
         drain(xg.at[c, 0], fs.at[c])
         drain(xg.at[c, 0], vs.at[c])
@@ -399,31 +406,26 @@
     pltpu.make_async_copy(hand, hand_hbm, hs).wait()
 
 
-def slots(owners, lengths, target):
-    p = jnp.arange(PROMPTS, dtype=jnp.int32)
-    same = (owners[..., :, None] == owners[..., None, :]) & (p[None, :] < p[:, None])
-    rank = jnp.sum(same.astype(jnp.int32), axis=-1)
-    hit = (owners[..., None, None, :] == target[..., :, None, None]) & (
-        rank[..., None, None, :] == jnp.arange(2, dtype=jnp.int32)[:, None]
+def slots(owner, lengths, inst, head):
+    take = lambda v: jnp.concatenate(
+        [lax.dynamic_slice(v, (inst * PROMPTS,), (PROMPTS,)), lax.dynamic_slice(v, (head * 96,), (96,))]
     )
-    return jnp.sum(jnp.where(hit, (p * 256 + lengths)[..., None, None, :], 0), axis=-1)
+    who, lens = take(owner.reshape(-1)), take(lengths)
+    p, t = jnp.arange(120, dtype=jnp.int32), jnp.arange(72, dtype=jnp.int32)
+    group = p // PROMPTS
+    rank = jnp.sum(
+        ((who[:, None] == who[None, :]) & (group[:, None] == group[None, :]) & (p[None, :] < p[:, None])).astype(jnp.int32),
+        axis=1,
+    )
+    target = jnp.where(t < 64, t // 2, inst)
+    part = jnp.where(t < 64, 0, t // 2 - 31)
+    hit = (who[None, :] == target[:, None]) & (group[None, :] == part[:, None]) & (rank[None, :] == (t % 2)[:, None])
+    return jnp.sum(jnp.where(hit, (p % PROMPTS * 256 + lens)[None, :], 0), axis=1)
 
 
 def local(kv_cache, query, fresh_kv, lengths, owner, tokens, expert_ids, gate_weights, w_gate, w_up, w_down):
     inst, head = lax.axis_index("inst"), lax.axis_index("head")
-    owners, lens = owner[:, 0].reshape(32, PROMPTS), lengths.reshape(32, PROMPTS)
-    own_o = lax.dynamic_index_in_dim(owners, inst, 0, keepdims=False)
-    own_l = lax.dynamic_index_in_dim(lens, inst, 0, keepdims=False)
-    sends = slots(own_o, own_l, jnp.arange(32, dtype=jnp.int32))
-    src_o = lax.dynamic_slice_in_dim(owners, head * 4, 4, 0)
-    src_l = lax.dynamic_slice_in_dim(lens, head * 4, 4, 0)
-    gets = slots(src_o, src_l, jnp.broadcast_to(inst, (4, 1)))
-    codes = jnp.concatenate([sends.reshape(64), gets.reshape(8)])
-
-    z = lax.rem(inst, 8) // 2 * 2 + lax.rem(head, 2)
-    route = jnp.concatenate([expert_ids.T.astype(F32), gate_weights.T], axis=0)
-    lane = jnp.arange(COL, dtype=jnp.int32)
-    route = jnp.where(lane[None, :] // TOK == z, jnp.tile(route, (1, NZ)), 0.0)
+    codes = slots(owner, lengths, inst, head)
 
     kv = jnp.swapaxes(kv_cache, 2, 3).reshape(PROMPTS, 128, 128)
     qf = jnp.concatenate([query.reshape(PROMPTS, 8, 128), fresh_kv[:, None, :]], axis=1)
@@ -438,9 +440,10 @@
             jax.ShapeDtypeStruct((8, 64 * 128), BF16),
             jax.ShapeDtypeStruct((TOK, D), BF16),
         ),
-        in_specs=[smem] + [vmem] * 4 + [hbm] * 3,
+        in_specs=[smem] + [vmem] * 5 + [hbm] * 3,
         out_specs=(hbm, vmem, vmem),
         scratch_shapes=[
+            pltpu.VMEM((16, COL), F32),
             pltpu.VMEM((NZ, 16, COL), F32),
             pltpu.VMEM((2, 4, 16, COL), F32),
             pltpu.VMEM((NCH, 4, COL, DC), BF16),
@@ -475,7 +478,7 @@
             collective_id=1, has_side_effects=True, vmem_limit_bytes=58 * 2**20
         ),
     )(
-        codes, route, tokens, kv, qf,
+        codes, expert_ids.T, gate_weights.T, tokens, kv, qf,
         w_gate, w_up, w_down,
     )
     return handed, att, moe

time: 183 us -> 173 us (0.945); the launches traced: 179 us -> 172 us
  Pallas kernels: 167 us -> 162 us
  other arithmetic: 4.73 us -> 1.72 us
    pallas_call x1, Pallas kernels: 167 us -> 162 us  [local(): pl.pallas_call(kernel, out_shape=(jax.ShapeDtypeStruct((8, 2, 128, 512),...]
    unnamed x8 -> x10, local copies, waits for them, and re-layouts: 5.26 us -> 5.27 us
where the time goes in v3:
time: 173 us; the launch traced here: 172 us
  Pallas kernels  162 us (94%)
  local copies, waits for them, and re-layouts  7.65 us (4%)
    pallas_call x1, Pallas kernels, local(): pl.pallas_call(kernel, out_shape=(jax.ShapeDtypeStruct((8, 2, 128, 512),...  162 us
    unnamed x10, local copies, waits for them, and re-layouts  5.27 us

profile of v3, /device:TPU:2, one launch (start us, length us, event | category | flops | bytes accessed | tf_op | source)
XLA Modules:
  0.0 171.9 jit_solution(13678679081776527732)
XLA Ops:
  0.6 0.0 copy-start
  0.7 0.8 dynamic_slice.21
  1.4 0.0 copy-done
  1.4 0.1 dynamic-slice_bitcast_fusion
  1.5 0.8 dynamic_slice.20
  2.3 0.1 dynamic-slice_bitcast_fusion.1
  2.3 0.1 pad_add_fusion
  2.4 0.1 and_select_fusion.2
  2.5 0.2 convert_reduce_fusion
  2.7 0.7 select_reduce_fusion.code_sm
  3.4 0.7 copy.15
  4.1 0.8 copy.16
  4.9 0.7 fusion.2.qf
  5.6 161.9 %shard_map.130 = (bf16[8,2,128,512]{3,2,1,0:T(8,128)(2,1)}, bf16[8,8192]{1,0:T(8,128)(2,1)}, bf16[16,4096]{1,0:T(8,128)(2,1)}) custom-call(s32[72]{0:T(128)} %select_reduce_fusion.code_sm, s32[8,16]{1,0:T(8,128)} %bitcast.16, f32[8,16]{1,0:T(8,128)} %bitcast.17, bf16[16,4096]{1,0:T(8,128)(2,1)} %tok.1, bf16[24,128,128]{2,1,0:T(8,128)(2,1)} %bitcast.12, ...), custom_call_target="tpu_custom_call" | custom-call | tf_op jit(solution)/shard_map/pallas_call | solution.py:436
  167.5 0.0 copy-start.2
  167.5 0.0 copy-start.1
  167.5 3.1 %copy.20 = bf16[8,2,128,512]{3,2,1,0:T(8,128)(2,1)} copy(bf16[8,2,128,512]{3,2,1,0:T(8,128)(2,1)} %get-tuple-element.10) | data formatting | bytes 4194304
  170.6 0.0 copy-done.2
  170.6 0.7 copy.21
  171.3 0.0 copy-done.1
  171.3 0.7 copy.22
  (2 shorter events, 0.0 us)
Async XLA Ops:
  0.6 0.8 copy-start
  167.5 3.2 %copy-start.2 = (bf16[8,8192]{1,0:T(8,128)(2,1)S(1)}, bf16[8,8192]{1,0:T(8,128)(2,1)}, u32[]{:S(2)}) copy-start(bf16[8,8192]{1,0:T(8,128)(2,1)} %get-tuple-element.11) | copy-start | bytes 393220
  167.5 3.8 %copy-start.1 = (bf16[16,4096]{1,0:T(8,128)(2,1)S(1)}, bf16[16,4096]{1,0:T(8,128)(2,1)}, u32[]{:S(2)}) copy-start(bf16[16,4096]{1,0:T(8,128)(2,1)} %get-tuple-element.12) | copy-start | bytes 393220
